TPU v7x, 1024 devices: a whole 4x4x32 slice. The times are simulated.
1024 devices in a mesh: gx: 8 (over y, core), gy: 16 (over z_hi, x), gz: 8 (over z_lo).
Axes of the slice: x: 4, y: 4, z: 32 (z_hi: 4, z_lo: 8; z = z_hi * 8 + z_lo), core: 2. Of those that a mesh axis runs over, the one named last changes fastest.
Arguments:
- source: float32 [128, 256, 1024], P('gx', 'gy', 'gz'), may hold values from -48 to 48, as said below
- metric_xx: float32 [128, 256, 1024], P('gx', 'gy', 'gz'), may hold values from 0.004 to 0.04
- metric_yy: float32 [128, 256, 1024], P('gx', 'gy', 'gz'), may hold values from 0.004 to 0.04
- metric_zz: float32 [128, 256, 1024], P('gx', 'gy', 'gz'), may hold values from 0.004 to 0.04
- mass_term: float32 [128, 256, 1024], P('gx', 'gy', 'gz'), may hold values from 0.3 to 3
Outputs:
- solution: float32 [128, 256, 1024], P('gx', 'gy', 'gz')
- residual: float32 [128, 256, 1024], P('gx', 'gy', 'gz')
Inputs may be any that keep to these rules, and one draw needn't show every extreme that they name: `source`: element-local loads; not continuous across elements.
All inputs are finite; a program needn't handle non-finite values.
Results may differ from a plain program's by a relative error of at most 0.0003.
Values sent between devices are 32-bit elements; how exact they have to be, the bound alone decides.
A program may use at most 32 MiB of HBM per device.

v0:
```python
import jax
import jax.numpy as jnp
import numpy as np
from jax import lax
from jax.sharding import PartitionSpec as P

ITERS = 4


def with_halo(cells, sides, width):
    for axis, dim in sides:
        count = lax.axis_size(axis)
        ends = count - 1
        head = lax.slice_in_dim(cells, 0, width, axis=dim)
        tail = lax.slice_in_dim(cells, cells.shape[dim] - width, cells.shape[dim], axis=dim)
        cells = jnp.concatenate(
            [
                lax.ppermute(tail, axis, [(i, (i + 1) % count) for i in range(ends)]),
                cells,
                lax.ppermute(head, axis, [((i + 1) % count, i) for i in range(ends)]),
            ],
            axis=dim,
        )
    return cells


def derivative_table():
    points = np.array(
        [
            -1.0,
            -0.8717401485096066,
            -0.5917001814331423,
            -0.2092992179024789,
            0.2092992179024789,
            0.5917001814331423,
            0.8717401485096066,
            1.0,
        ]
    )
    weights_c = np.array(
        [
            np.prod(
                [
                    points[row_index] - points[col_index]
                    for col_index in range(8)
                    if col_index != row_index
                ]
            )
            for row_index in range(8)
        ]
    )
    table = np.zeros((8, 8))
    for row_index in range(8):
        for col_index in range(8):
            if row_index != col_index:
                table[row_index, col_index] = weights_c[row_index] / (
                    weights_c[col_index] * (points[row_index] - points[col_index])
                )
        table[row_index, row_index] = -np.sum(table[row_index])
    return jnp.asarray(table, jnp.float32)


def apply_along(field, matrix, which_dim):
    extent_x, extent_y, extent_z = field.shape
    if which_dim == 0:
        blocks = field.reshape(extent_x // 8, 8, extent_y, extent_z)
        result = jnp.einsum("ki,aibc->akbc", matrix, blocks, precision=lax.Precision.HIGHEST)
    elif which_dim == 1:
        blocks = field.reshape(extent_x, extent_y // 8, 8, extent_z)
        result = jnp.einsum("ki,abic->abkc", matrix, blocks, precision=lax.Precision.HIGHEST)
    else:
        blocks = field.reshape(extent_x, extent_y, extent_z // 8, 8)
        result = jnp.einsum("ki,abci->abck", matrix, blocks, precision=lax.Precision.HIGHEST)
    return result.reshape(field.shape)


def local_apply(field, derivative, metric_xx, metric_yy, metric_zz, mass_term):
    total = mass_term * field
    for which_dim, factor in ((0, metric_xx), (1, metric_yy), (2, metric_zz)):
        slope = apply_along(field, derivative, which_dim)
        total = total + apply_along(factor * slope, derivative.T, which_dim)
    return total


def local_diagonal(derivative, metric_xx, metric_yy, metric_zz, mass_term):
    squared = (derivative * derivative).T
    total = mass_term
    for which_dim, factor in ((0, metric_xx), (1, metric_yy), (2, metric_zz)):
        total = total + apply_along(factor, squared, which_dim)
    return total


def pair_sum(padded, which_dim):
    extent = padded.shape[which_dim] - 2
    middle = lax.slice_in_dim(padded, 1, extent + 1, axis=which_dim)
    following = lax.slice_in_dim(padded, 2, extent + 2, axis=which_dim)
    previous = lax.slice_in_dim(padded, 0, extent, axis=which_dim)
    within = lax.iota(jnp.int32, extent) % 8
    layout = [1, 1, 1]
    layout[which_dim] = extent
    closing = (within == 7).reshape(layout)
    opening = (within == 0).reshape(layout)
    return middle + jnp.where(closing, following, 0.0) + jnp.where(opening, previous, 0.0)


def copies(extent, offset, total):
    slots = offset + lax.iota(jnp.int32, extent)
    more = jnp.where((slots % 8 == 7) & (slots != total - 1), 1.0, 0.0)
    more = more + jnp.where((slots % 8 == 0) & (slots != 0), 1.0, 0.0)
    return (1.0 + more).astype(jnp.float32)


def assemble(field):
    padded = with_halo(field, (("gx", 0), ("gy", 1), ("gz", 2)), 1)
    return pair_sum(pair_sum(pair_sum(padded, 0), 1), 2)


def shards(source, metric_xx, metric_yy, metric_zz, mass_term):
    derivative = derivative_table()
    extent_x, extent_y, extent_z = source.shape
    copies_x = copies(extent_x, lax.axis_index("gx") * extent_x, extent_x * lax.axis_size("gx"))
    copies_y = copies(extent_y, lax.axis_index("gy") * extent_y, extent_y * lax.axis_size("gy"))
    copies_z = copies(extent_z, lax.axis_index("gz") * extent_z, extent_z * lax.axis_size("gz"))
    weights = 1.0 / (copies_x[:, None, None] * copies_y[None, :, None] * copies_z[None, None, :])
    jacobi = 1.0 / assemble(local_diagonal(derivative, metric_xx, metric_yy, metric_zz, mass_term))

    def operator(field):
        return assemble(local_apply(field, derivative, metric_xx, metric_yy, metric_zz, mass_term))

    solution = jnp.zeros_like(source)
    residual = assemble(source)
    smoothed = jacobi * residual
    image = operator(smoothed)
    search = jnp.zeros_like(source)
    search_img = jnp.zeros_like(source)
    search_pre = jnp.zeros_like(source)
    search_op = jnp.zeros_like(source)
    gamma_old = jnp.float32(1.0)
    alpha_old = jnp.float32(1.0)
    for iteration in range(ITERS):
        gamma_now, delta_now = lax.psum(
            (jnp.sum(weights * residual * smoothed), jnp.sum(weights * image * smoothed)),
            ("gx", "gy", "gz"),
        )
        image_pre = jacobi * image
        image_op = operator(image_pre)
        if iteration == 0:
            beta_now = jnp.float32(0.0) * gamma_now
            alpha_now = gamma_now / delta_now
        else:
            beta_now = gamma_now / gamma_old
            alpha_now = gamma_now / (delta_now - beta_now * gamma_now / alpha_old)
        search_op = image_op + beta_now * search_op
        search_pre = image_pre + beta_now * search_pre
        search_img = image + beta_now * search_img
        search = smoothed + beta_now * search
        solution = solution + alpha_now * search
        residual = residual - alpha_now * search_img
        smoothed = smoothed - alpha_now * search_pre
        image = image - alpha_now * search_op
        gamma_old = gamma_now
        alpha_old = alpha_now
    return (solution, residual)


def solution(mesh):
    return jax.shard_map(
        shards,
        mesh=mesh,
        in_specs=(
            P("gx", "gy", "gz"),
            P("gx", "gy", "gz"),
            P("gx", "gy", "gz"),
            P("gx", "gy", "gz"),
            P("gx", "gy", "gz"),
        ),
        out_specs=(P("gx", "gy", "gz"), P("gx", "gy", "gz")),
        check_vma=False,
    )
```

profile of v0, /device:TPU:1, one launch (start us, length us, event | category | flops | bytes accessed | tf_op | source)
XLA Modules:
  0.0 887.7 jit_solution(7451291067145981666)
XLA Ops:
  7.3 16.1 %collective-permute-start.7 = (f32[1,16,128]{2,1,0:T(8,128)S(1)}, f32[1,16,128]{2,1,0:T(8,128)S(1)}, u32[]{:S(2)}, u32[]{:S(2)}) collective-permute-start(f32[1,16,128]{2,1,0:T(8,128)S(1)} %get-tuple-element.66), channel_id=1, source_target_pairs={{128,0},{256,128},{384,256},{512,384},{640,512},{768,640},{896,768... | collective-permute-start | bytes 24584 | tf_op jit(solution)/shard_map/ppermute | solution.py:20
  23.3 1.9 collective-permute-start.6
  25.3 1.9 collective-permute-start
  27.2 2.4 collective-permute-start.1
  31.0 4.0 collective-permute-start.8
  36.4 4.0 collective-permute-start.2
  41.9 4.0 collective-permute-start.10
  46.1 1.3 collective-permute-start.5
  47.4 4.0 collective-permute-start.4
  51.7 2.5 collective-permute-done.5
  60.0 4.2 collective-permute-start.13
  64.2 3.2 collective-permute-start.12
  69.5 4.0 collective-permute-start.14
  75.8 4.9 collective-permute-start.16
  80.7 3.3 collective-permute-done.17
  91.9 3.1 collective-permute-start.19
  95.0 3.4 collective-permute-start.18
  100.5 4.5 collective-permute-start.20
  107.3 4.7 collective-permute-start.22
  112.0 215.4 %all-reduce.3 = (f32[]{:T(128)}, f32[]{:T(128)}) all-reduce(f32[]{:T(128)} %get-tuple-element.9, f32[]{:T(128)} %get-tuple-element.8), channel_id=1, replica_groups=mesh['gx'=8,'gy'=16,'gz'=8] {'gx','gy','gz'}, use_global_device_ids=true, to_apply=%region_1.2 | all-reduce | flops 2 | bytes 16 | tf_op jit(solution)/shard_map/psum | solution.py:141
  336.8 3.0 collective-permute-start.25
  339.8 2.6 collective-permute-start.24
  344.5 4.0 collective-permute-start.26
  350.8 4.7 collective-permute-start.28
  356.2 167.9 %all-reduce.2 = (f32[]{:T(128)}, f32[]{:T(128)}) all-reduce(f32[]{:T(128)} %get-tuple-element.7, f32[]{:T(128)} %get-tuple-element.6), channel_id=1, replica_groups=mesh['gx'=8,'gy'=16,'gz'=8] {'gx','gy','gz'}, use_global_device_ids=true, to_apply=%region_5.6 | all-reduce | flops 2 | bytes 16 | tf_op jit(solution)/shard_map/psum | solution.py:141
  530.9 1.6 multiply_reduce_fusion.2
  536.5 2.8 collective-permute-start.31
  539.3 2.7 collective-permute-start.30
  544.1 4.0 collective-permute-start.32
  550.4 4.0 collective-permute-start.34
  554.4 170.7 %all-reduce.1 = (f32[]{:T(128)}, f32[]{:T(128)}) all-reduce(f32[]{:T(128)} %get-tuple-element.5, f32[]{:T(128)} %get-tuple-element.4), channel_id=1, replica_groups=mesh['gx'=8,'gy'=16,'gz'=8] {'gx','gy','gz'}, use_global_device_ids=true, to_apply=%region_9.10 | all-reduce | flops 2 | bytes 16 | tf_op jit(solution)/shard_map/psum | solution.py:141
  731.2 151.3 %all-reduce = (f32[]{:T(128)}, f32[]{:T(128)}) all-reduce(f32[]{:T(128)} %get-tuple-element.3, f32[]{:T(128)} %get-tuple-element.2), channel_id=1, replica_groups=mesh['gx'=8,'gy'=16,'gz'=8] {'gx','gy','gz'}, use_global_device_ids=true, to_apply=%region_13.14 | all-reduce | flops 2 | bytes 16 | tf_op jit(solution)/shard_map/psum | solution.py:141
  (197 shorter events, 59.9 us)
Async XLA Ops:
  7.3 22.4 %collective-permute-start.7 = (f32[1,16,128]{2,1,0:T(8,128)S(1)}, f32[1,16,128]{2,1,0:T(8,128)S(1)}, u32[]{:S(2)}, u32[]{:S(2)}) collective-permute-start(f32[1,16,128]{2,1,0:T(8,128)S(1)} %get-tuple-element.66), channel_id=1, source_target_pairs={{128,0},{256,128},{384,256},{512,384},{640,512},{768,640},{896,768... | collective-permute-start | bytes 24584 | tf_op jit(solution)/shard_map/ppermute | solution.py:20
  23.3 6.3 collective-permute-start.6
  25.3 9.7 %collective-permute-start = (f32[1,16,128]{2,1,0:T(8,128)S(1)}, f32[1,16,128]{2,1,0:T(8,128)S(1)}, u32[]{:S(2)}, u32[]{:S(2)}) collective-permute-start(f32[1,16,128]{2,1,0:T(8,128)S(1)} %get-tuple-element.68), channel_id=1, source_target_pairs={{0,128},{128,256},{256,384},{384,512},{512,640},{640,768},{768,896... | collective-permute-start | bytes 24584 | tf_op jit(solution)/shard_map/ppermute | solution.py:18
  27.2 7.8 collective-permute-start.1
  29.7 10.7 %collective-permute-start.9 = (f32[18,1,128]{2,1,0:T(1,128)S(1)}, f32[18,1,128]{2,1,0:T(1,128)S(1)}, u32[]{:S(2)}, u32[]{:S(2)}) collective-permute-start(f32[18,1,128]{2,1,0:T(1,128)S(1)} %get-tuple-element.54), channel_id=1, source_target_pairs={{8,0},{16,8},{24,16},{32,24},{40,32},{48,40},{56,48},{64,56},{72,6... | collective-permute-start | bytes 27656 | tf_op jit(solution)/shard_map/ppermute | solution.py:20
  31.0 9.4 %collective-permute-start.8 = (f32[18,1,128]{2,1,0:T(1,128)S(1)}, f32[18,1,128]{2,1,0:T(1,128)S(1)}, u32[]{:S(2)}, u32[]{:S(2)}) collective-permute-start(f32[18,1,128]{2,1,0:T(1,128)S(1)} %get-tuple-element.53), channel_id=1, source_target_pairs={{0,8},{8,16},{16,24},{24,32},{32,40},{40,48},{48,56},{56,64},{64,7... | collective-permute-start | bytes 27656 | tf_op jit(solution)/shard_map/ppermute | solution.py:18
  35.1 10.8 %collective-permute-start.3 = (f32[18,1,128]{2,1,0:T(1,128)S(1)}, f32[18,1,128]{2,1,0:T(1,128)S(1)}, u32[]{:S(2)}, u32[]{:S(2)}) collective-permute-start(f32[18,1,128]{2,1,0:T(1,128)S(1)} %get-tuple-element.56), channel_id=1, source_target_pairs={{8,0},{16,8},{24,16},{32,24},{40,32},{48,40},{56,48},{64,56},{72,6... | collective-permute-start | bytes 27656 | tf_op jit(solution)/shard_map/ppermute | solution.py:20
  36.4 9.5 %collective-permute-start.2 = (f32[18,1,128]{2,1,0:T(1,128)S(1)}, f32[18,1,128]{2,1,0:T(1,128)S(1)}, u32[]{:S(2)}, u32[]{:S(2)}) collective-permute-start(f32[18,1,128]{2,1,0:T(1,128)S(1)} %get-tuple-element.55), channel_id=1, source_target_pairs={{0,8},{8,16},{16,24},{24,32},{32,40},{40,48},{48,56},{56,64},{64,7... | collective-permute-start | bytes 27656 | tf_op jit(solution)/shard_map/ppermute | solution.py:18
  40.6 10.8 %collective-permute-start.11 = (f32[18,18,1]{2,1,0:T(8,128)S(1)}, f32[18,18,1]{2,1,0:T(8,128)S(1)}, u32[]{:S(2)}, u32[]{:S(2)}) collective-permute-start(f32[18,18,1]{2,1,0:T(8,128)S(1)} %get-tuple-element.42), channel_id=1, source_target_pairs={{1,0},{2,1},{3,2},{4,3},{5,4},{6,5},{7,6},{9,8},{10,9},{11,10},{12... | collective-permute-start | bytes 3896 | tf_op jit(solution)/shard_map/ppermute | solution.py:20
  41.9 9.5 %collective-permute-start.10 = (f32[18,18,1]{2,1,0:T(8,128)S(1)}, f32[18,18,1]{2,1,0:T(8,128)S(1)}, u32[]{:S(2)}, u32[]{:S(2)}) collective-permute-start(f32[18,18,1]{2,1,0:T(8,128)S(1)} %get-tuple-element.41), channel_id=1, source_target_pairs={{0,1},{1,2},{2,3},{3,4},{4,5},{5,6},{6,7},{8,9},{9,10},{10,11},{11... | collective-permute-start | bytes 3896 | tf_op jit(solution)/shard_map/ppermute | solution.py:18
  46.1 8.1 collective-permute-start.5
  47.4 7.4 collective-permute-start.4
  60.0 7.4 collective-permute-start.13
  68.2 5.4 collective-permute-start.15
  69.5 4.8 collective-permute-start.14
  74.5 9.6 %collective-permute-start.17 = (f32[18,18,1]{2,1,0:T(8,128)S(1)}, f32[18,18,1]{2,1,0:T(8,128)S(1)}, u32[]{:S(2)}, u32[]{:S(2)}) collective-permute-start(f32[18,18,1]{2,1,0:T(8,128)S(1)} %get-tuple-element.40), channel_id=1, source_target_pairs={{1,0},{2,1},{3,2},{4,3},{5,4},{6,5},{7,6},{9,8},{10,9},{11,10},{12... | collective-permute-start | bytes 3896 | tf_op jit(solution)/shard_map/ppermute | solution.py:20
  75.8 9.2 %collective-permute-start.16 = (f32[18,18,1]{2,1,0:T(8,128)S(1)}, f32[18,18,1]{2,1,0:T(8,128)S(1)}, u32[]{:S(2)}, u32[]{:S(2)}) collective-permute-start(f32[18,18,1]{2,1,0:T(8,128)S(1)} %get-tuple-element.39), channel_id=1, source_target_pairs={{0,1},{1,2},{2,3},{3,4},{4,5},{5,6},{6,7},{8,9},{9,10},{10,11},{11... | collective-permute-start | bytes 3896 | tf_op jit(solution)/shard_map/ppermute | solution.py:18
  91.9 6.5 collective-permute-start.19
  99.2 5.9 collective-permute-start.21
  100.5 5.3 collective-permute-start.20
  106.0 223.2 %collective-permute-start.23 = (f32[18,18,1]{2,1,0:T(8,128)S(1)}, f32[18,18,1]{2,1,0:T(8,128)S(1)}, u32[]{:S(2)}, u32[]{:S(2)}) collective-permute-start(f32[18,18,1]{2,1,0:T(8,128)S(1)} %get-tuple-element.38), channel_id=1, source_target_pairs={{1,0},{2,1},{3,2},{4,3},{5,4},{6,5},{7,6},{9,8},{10,9},{11,10},{12... | collective-permute-start | bytes 3896 | tf_op jit(solution)/shard_map/ppermute | solution.py:20
  107.3 221.9 %collective-permute-start.22 = (f32[18,18,1]{2,1,0:T(8,128)S(1)}, f32[18,18,1]{2,1,0:T(8,128)S(1)}, u32[]{:S(2)}, u32[]{:S(2)}) collective-permute-start(f32[18,18,1]{2,1,0:T(8,128)S(1)} %get-tuple-element.37), channel_id=1, source_target_pairs={{0,1},{1,2},{2,3},{3,4},{4,5},{5,6},{6,7},{8,9},{9,10},{10,11},{11... | collective-permute-start | bytes 3896 | tf_op jit(solution)/shard_map/ppermute | solution.py:18
  336.8 5.6 collective-permute-start.25
  343.2 5.3 collective-permute-start.27
  344.5 4.8 collective-permute-start.26
  349.5 179.1 %collective-permute-start.29 = (f32[18,18,1]{2,1,0:T(8,128)S(1)}, f32[18,18,1]{2,1,0:T(8,128)S(1)}, u32[]{:S(2)}, u32[]{:S(2)}) collective-permute-start(f32[18,18,1]{2,1,0:T(8,128)S(1)} %get-tuple-element.36), channel_id=1, source_target_pairs={{1,0},{2,1},{3,2},{4,3},{5,4},{6,5},{7,6},{9,8},{10,9},{11,10},{12... | collective-permute-start | bytes 3896 | tf_op jit(solution)/shard_map/ppermute | solution.py:20
  350.8 177.8 %collective-permute-start.28 = (f32[18,18,1]{2,1,0:T(8,128)S(1)}, f32[18,18,1]{2,1,0:T(8,128)}, u32[]{:S(2)}, u32[]{:S(2)}) collective-permute-start(f32[18,18,1]{2,1,0:T(8,128)S(1)} %get-tuple-element.35), channel_id=1, source_target_pairs={{0,1},{1,2},{2,3},{3,4},{4,5},{5,6},{6,7},{8,9},{9,10},{10,11},{11... | collective-permute-start | bytes 3896 | tf_op jit(solution)/shard_map/ppermute | solution.py:18
  536.5 5.6 collective-permute-start.31
  542.8 5.3 collective-permute-start.33
  544.1 4.8 collective-permute-start.32
  549.1 179.8 %collective-permute-start.35 = (f32[18,18,1]{2,1,0:T(8,128)S(1)}, f32[18,18,1]{2,1,0:T(8,128)S(1)}, u32[]{:S(2)}, u32[]{:S(2)}) collective-permute-start(f32[18,18,1]{2,1,0:T(8,128)S(1)} %get-tuple-element.34), channel_id=1, source_target_pairs={{1,0},{2,1},{3,2},{4,3},{5,4},{6,5},{7,6},{9,8},{10,9},{11,10},{12... | collective-permute-start | bytes 3896 | tf_op jit(solution)/shard_map/ppermute | solution.py:20
  550.4 178.5 %collective-permute-start.34 = (f32[18,18,1]{2,1,0:T(8,128)S(1)}, f32[18,18,1]{2,1,0:T(8,128)S(1)}, u32[]{:S(2)}, u32[]{:S(2)}) collective-permute-start(f32[18,18,1]{2,1,0:T(8,128)S(1)} %get-tuple-element.33), channel_id=1, source_target_pairs={{0,1},{1,2},{2,3},{3,4},{4,5},{5,6},{6,7},{8,9},{9,10},{10,11},{11... | collective-permute-start | bytes 3896 | tf_op jit(solution)/shard_map/ppermute | solution.py:18
  (23 other events, 390.5 us)
where the time goes:
time: 890 us; the launch traced here: 888 us
  blocking collectives  705 us (79%)
  starting transfers between devices  114 us (13%)
  between operations  15.6 us (2%)
  matrix products  14.8 us (2%)
  local copies, waits for them, and re-layouts  13.7 us (2%)
  waiting for transfers between devices  13.3 us (1%)
  other arithmetic  11.2 us (1%)
    psum x4, blocking collectives, shards(): lax.psum((jnp.sum(weights * residual * smoothed), jnp.sum(weights * image...  705 us
    ppermute x18, starting transfers between devices, with_halo(): lax.ppermute(tail, axis, [(i, (i + 1) % count) for i in range(ends)])  66.6 us
    ppermute x18, starting transfers between devices, with_halo(): lax.ppermute(head, axis, [((i + 1) % count, i) for i in range(ends)])  47.1 us
  transfers between devices with their start and end apart: 36, of which 12 were waited for; matrix products, arithmetic and copies ran while one was open for 0% of the time, Pallas kernels for 0%

commit v1 on v0

v1 whole, which is shorter than its diff:
```python
import itertools

import jax
import jax.numpy as jnp
import numpy as np
from jax import lax
from jax.experimental import pallas as pl
from jax.experimental.pallas import tpu as pltpu
from jax.sharding import PartitionSpec as P

MESH = pl.DeviceIdType.MESH
ITERS = 4
CENTRE, HALF = 1.2, 1.1
AXES = ("gx", "gy", "gz")

NEAR = sorted(
    (o for o in itertools.product((-1, 0, 1), repeat=3) if o != (0, 0, 0)),
    key=lambda o: (o[1] == 0, -abs(o[0]) - abs(o[2])),
)


def derivative_table():
    points = np.array(
        [
            -1.0,
            -0.8717401485096066,
            -0.5917001814331423,
            -0.2092992179024789,
            0.2092992179024789,
            0.5917001814331423,
            0.8717401485096066,
            1.0,
        ]
    )
    gaps = points[:, None] - points[None, :] + np.eye(8)
    weights_c = np.prod(gaps, axis=1)
    table = weights_c[:, None] / (weights_c[None, :] * gaps)
    table = table - np.diag(np.diag(table))
    return table - np.diag(table.sum(axis=1))


TABLE = derivative_table()


def sublane_factors(matrix):
    k = np.arange(8)
    rows = np.stack([matrix[k, (k + s) % 8] for s in range(8)])
    return np.repeat(rows[:, :, None], 128, axis=2)


def constants():
    square = (TABLE * TABLE).T
    mats = [np.kron(np.eye(16), m.T) for m in (TABLE, TABLE.T, square)]
    facs = [sublane_factors(m) for m in (TABLE, TABLE.T, square)]
    return np.stack(mats).astype(np.float32), np.stack(facs).astype(np.float32)


def along_x(field, matrix):
    out = [None] * 16
    for base in (0, 8):
        even = [field[base + i] + field[base + 7 - i] for i in range(4)]
        odd = [field[base + i] - field[base + 7 - i] for i in range(4)]
        for k in range(4):
            e = sum(float(0.5 * (matrix[k, i] + matrix[k, 7 - i])) * even[i] for i in range(4))
            o = sum(float(0.5 * (matrix[k, i] - matrix[k, 7 - i])) * odd[i] for i in range(4))
            out[base + k] = o + e
            out[base + 7 - k] = o - e
    return out


def along_x_plain(field, matrix):
    return [
        sum(float(matrix[k % 8, i]) * field[k // 8 * 8 + i] for i in range(8)) for k in range(16)
    ]


def along_y(field, facs):
    total = field * facs[0][None]
    for s in range(1, 8):
        total = total + pltpu.roll(field, 8 - s, 1) * facs[s][None]
    return total


def along_z(field, mat):
    flat = field.reshape(256, 128)
    return jnp.dot(flat, mat, precision=lax.Precision.HIGHEST, preferred_element_type=jnp.float32)


def slabs(field):
    return [field[i] for i in range(16)]


def kernel(
    dims, xwidth,
    src_ref, mx_ref, my_ref, mz_ref, mass_ref, mats_ref, facs_ref,
    sol_ref, res_ref,
    jac, T, L, V, Z, A, YS, PS, XF, YF, ZF, XZ, RB, acc, row_a, row_b, buf_a, buf_b,
    ssem, rsem, ssem_a, rsem_a, ssem_b, rsem_b,
):
    nx, ny, nz = dims
    ix, iy, iz = (lax.axis_index(a) for a in AXES)
    here = {0: (ix, nx), 1: (iy, ny), 2: (iz, nz)}

    def exists(o):
        ok = None
        for d in range(3):
            at, n = here[d]
            c = at > 0 if o[d] < 0 else at < n - 1 if o[d] > 0 else None
            ok = c if ok is None else ok if c is None else jnp.logical_and(ok, c)
        return ok

    def dev(o):
        return (ix + o[0], iy + o[1], iz + o[2])

    depth = ny // xwidth
    plane, ring = nx * xwidth, depth * nz
    my_a = ix * xwidth + lax.rem(iy, xwidth)
    my_b = (iy // xwidth) * nz + iz

    def dev_a(k):
        to = lax.rem(my_a + k, plane)
        return (to // xwidth, (iy // xwidth) * xwidth + lax.rem(to, xwidth), iz)

    def dev_b(k):
        to = lax.rem(my_b + k, ring)
        return (ix, (to // nz) * xwidth + lax.rem(iy, xwidth), lax.rem(to, nz))

    def far_first(i, n):
        half = (i + 1) // 2
        return n // 2 + jnp.where(lax.rem(i, 2) == 1, half, -half)

    for ref in (XF, YF, ZF, XZ, RB):
        ref[...] = jnp.zeros_like(ref)
    barrier = pltpu.get_barrier_semaphore()

    def greet(group, n):
        def body(i, c):
            pl.semaphore_signal(barrier, inc=1, device_id=group(far_first(i, n)), device_id_type=MESH)
            return c
        lax.fori_loop(0, n - 1, body, 0)

    greet(dev_b, ring)
    for o in NEAR:
        @pl.when(exists(o))
        def _(o=o):
            pl.semaphore_signal(barrier, inc=1, device_id=dev(o), device_id_type=MESH)
    greet(dev_a, plane)
    sides = [1 + (at > 0).astype(jnp.int32) + (at < n - 1).astype(jnp.int32) for at, n in here.values()]
    n_near = sides[0] * sides[1] * sides[2] - 1

    lane = lax.broadcasted_iota(jnp.int32, (8, 128), 1)
    sub = lax.broadcasted_iota(jnp.int32, (8, 128), 0)
    within = lax.rem(lane, 8)
    close = jnp.where((within == 7) & (lane != 127), 1.0, 0.0)[None]
    opens = jnp.where((within == 0) & (lane != 0), 1.0, 0.0)[None]
    even = lax.rem(lane, 2) == 0
    low = lax.rem(lane, 4) < 2
    ends_y = (low & (sub == 0)) | (jnp.logical_not(low) & (sub == 7))
    ends_z = (lane == 0) | (lane == 127)

    def prepare(s, f, raw):
        v = raw.reshape(32, 8, 128)
        v = v + pltpu.roll(v, 127, 2) * close + pltpu.roll(v, 1, 2) * opens
        t = T.at[s, f]
        t[...] = v.reshape(16, 16, 128)
        both = t[7] + t[8]
        t[7] = both
        t[8] = both
        both = t[:, 7, :] + t[:, 8, :]
        t[:, 7, :] = both
        t[:, 8, :] = both
        YS[s, f, 0] = t[:, 0, :]
        YS[s, f, 1] = t[:, 15, :]
        packed = jnp.zeros((8, 128), jnp.float32)
        for i in range(32):
            tile = t[i // 2, pl.ds(8 * (i % 2), 8), :]
            packed = jnp.where(lane // 2 == i, pltpu.roll(tile, 2 * i + 1, 1), packed)
        PS[s, f] = packed

    def end(d):
        return 0 if d < 0 else 1

    def copies(s, fields):
        fs = pl.ds(0, fields)
        for n, o in enumerate(NEAR):
            dx, dy, dz = o
            ex, ey, ez = end(-dx), end(-dy), end(-dz)
            edge = pl.ds(7 * end(dy), 1)
            if dz == 0:
                if dy == 0:
                    src, dst = T.at[s, fs, 15 * end(dx)], XF.at[s, fs, ex]
                elif dx == 0:
                    src, dst = YS.at[s, fs, end(dy)], YF.at[s, fs, ey]
                else:
                    src = YS.at[s, fs, end(dy), pl.ds(15 * end(dx), 1)]
                    dst = RB.at[s, fs, pl.ds(2 * ex + ey, 1)]
            elif dy == 0:
                src = PS.at[s, fs]
                dst = ZF.at[s, fs, ez] if dx == 0 else XZ.at[s, fs, 2 * ex + ez]
            else:
                src = PS.at[s, fs, edge]
                slot = 4 + 2 * ey + ez if dx == 0 else 8 + 4 * ex + 2 * ey + ez
                dst = RB.at[s, fs, pl.ds(slot, 1)]
            yield o, pltpu.make_async_remote_copy(
                src_ref=src, dst_ref=dst, send_sem=ssem.at[s, n], recv_sem=rsem.at[s, n],
                device_id=dev(o), device_id_type=MESH,
            )

    def send(s, fields):
        for o, copy in copies(s, fields):
            pl.when(exists(o))(copy.start)

    def receive(s, fields):
        order = {o: n for n, o in enumerate(NEAR)}
        for o, copy in copies(s, fields):
            back = tuple(-d for d in o)
            pl.when(exists(back))(copy.wait_recv)

    def sent(s, fields):
        for o, copy in copies(s, fields):
            pl.when(exists(o))(copy.wait_send)

    def merge(minus, plus):
        return jnp.where(even, pltpu.roll(plus, 127, 1), pltpu.roll(minus, 1, 1))

    def finish(s, f, out):
        rb = RB.at[s, f]

        def line(k):
            return jnp.broadcast_to(rb[pl.ds(k, 1), :], (8, 128))

        def with_y(m, first):
            minus = merge(line(first), line(first + 1))
            plus = merge(line(first + 2), line(first + 3))
            c = jnp.where(low, pltpu.roll(minus, 126, 1), pltpu.roll(plus, 2, 1))
            return m + jnp.where(ends_y, c, 0.0)

        m = with_y(merge(ZF[s, f, 0], ZF[s, f, 1]), 4)
        m_minus = with_y(merge(XZ[s, f, 0], XZ[s, f, 1]), 8)
        m_plus = with_y(merge(XZ[s, f, 2], XZ[s, f, 3]), 12)
        m = m + jnp.where(lane < 4, pltpu.roll(m_minus, 68, 1), 0.0)
        m = m + jnp.where((lane >= 60) & (lane < 64), pltpu.roll(m_plus, 60, 1), 0.0)
        for i in range(32):
            at = (i // 2, pl.ds(8 * (i % 2), 8), slice(None))
            part = jnp.where(ends_z, pltpu.roll(m, 127 - 2 * i, 1), 0.0)
            out[at] = T[(s, f) + at] + part
        out[:, 0, :] = out[:, 0, :] + YF[s, f, 0]
        out[:, 15, :] = out[:, 15, :] + YF[s, f, 1]
        for e in (0, 1):
            out[15 * e] = out[15 * e] + XF[s, f, e]
            for g in (0, 1):
                r = pl.ds(15 * g, 1)
                out[15 * e, r, :] = out[15 * e, r, :] + rb[pl.ds(2 * e + g, 1), :]

    def local(v):
        total = mass_ref[...] * v
        slope = along_x(slabs(v), TABLE)
        slope = [mx_ref[i] * slope[i] for i in range(16)]
        total = total + jnp.stack(along_x(slope, TABLE.T))
        v3 = v.reshape(32, 8, 128)
        slope = my_ref[...].reshape(32, 8, 128) * along_y(v3, facs_ref[0])
        total = total + along_y(slope, facs_ref[1]).reshape(16, 16, 128)
        slope = mz_ref[...].reshape(256, 128) * along_z(v, mats_ref[0])
        return total + along_z(slope, mats_ref[1]).reshape(16, 16, 128)

    def product(slot, a, b):
        acc[slot] = jnp.sum((a * b).reshape(32, 8, 128), axis=0)

    def products(j, count):
        for i in range(count):
            product(4 * j + i, L[...], V[i])
        product(16 + j, src_ref[...], V[j])

    diag = mass_ref[...] + jnp.stack(along_x_plain(slabs(mx_ref[...]), (TABLE * TABLE).T))
    diag = diag + along_y(my_ref[...].reshape(32, 8, 128), facs_ref[2]).reshape(16, 16, 128)
    diag = diag + along_z(mz_ref[...], mats_ref[2]).reshape(16, 16, 128)
    prepare(0, 0, src_ref[...])
    prepare(0, 1, diag)
    pl.semaphore_wait(barrier, n_near + (plane - 1) + (ring - 1))
    send(0, 2)
    V[...] = jnp.zeros_like(V)
    acc[...] = jnp.zeros_like(acc)
    Z[0] = jnp.zeros((16, 16, 128), jnp.float32)
    receive(0, 2)
    finish(0, 0, Z.at[1])
    finish(0, 1, jac)
    jac[...] = 1.0 / jac[...]
    V[0] = jac[...] * Z[1]

    def step(j, c):
        L[...] = local(V[j])
        prepare(j + 1, 0, L[...])
        send(j + 1, 1)
        products(j, ITERS)
        receive(j + 1, 1)
        finish(j + 1, 0, A.at[j])
        first = j == 0
        gain = jnp.where(first, 1.0 / HALF, 2.0 / HALF)
        z = gain * (A[j] - CENTRE * Z[j + 1]) - jnp.where(first, 0.0, 1.0) * Z[j]
        Z[j + 2] = z
        V[j + 1] = jac[...] * z
        return c

    lax.fori_loop(0, ITERS - 1, step, 0)

    last = ITERS - 1
    L[...] = local(V[last])
    products(last, ITERS)
    sums = jnp.sum(acc[...], axis=1)
    sums = jnp.sum(sums, axis=1, keepdims=True)
    pick = lax.broadcasted_iota(jnp.int32, (24, 128), 0) == lax.broadcasted_iota(jnp.int32, (24, 128), 1)

    def share(row, buf, me, group, n, ss, rs, values):
        row[...] = values
        buf[me] = values

        def copy(i):
            k = far_first(i, n)
            return pltpu.make_async_remote_copy(
                src_ref=row, dst_ref=buf.at[me], send_sem=ss.at[k], recv_sem=rs.at[k],
                device_id=group(k), device_id_type=MESH,
            )

        def begin(i, c):
            copy(i).start()
            return c

        def arrive(i, c):
            copy(i).wait_recv()
            return c

        def left(i, c):
            copy(i).wait_send()
            return c

        lax.fori_loop(0, n - 1, begin, 0)
        return lambda: lax.fori_loop(0, n - 1, arrive, 0), lambda: lax.fori_loop(0, n - 1, left, 0)

    values = jnp.sum(jnp.where(pick, sums, 0.0), axis=0, keepdims=True)
    arrive_a, left_a = share(row_a, buf_a, my_a, dev_a, plane, ssem_a, rsem_a, values)
    prepare(ITERS, 0, L[...])
    send(ITERS, 1)
    arrive_a()
    values = jnp.sum(buf_a[...], axis=0)
    arrive_b, left_b = share(row_b, buf_b, my_b, dev_b, ring, ssem_b, rsem_b, values)
    receive(ITERS, 1)
    finish(ITERS, 0, A.at[last])
    arrive_b()
    values = jnp.broadcast_to(jnp.sum(buf_b[...], axis=0), (8, 128))

    def value(k):
        return jnp.sum(jnp.where(lane == k, values, 0.0), axis=1, keepdims=True)

    H = [[value(4 * max(i, j) + min(i, j)) for j in range(ITERS)] for i in range(ITERS)]
    g = [value(16 + i) for i in range(ITERS)]
    for k in range(ITERS):
        inv = 1.0 / H[k][k]
        for i in range(k + 1, ITERS):
            f = H[i][k] * inv
            for j in range(k + 1, ITERS):
                H[i][j] = H[i][j] - f * H[k][j]
            g[i] = g[i] - f * g[k]
    y = [None] * ITERS
    for k in reversed(range(ITERS)):
        s = g[k]
        for j in range(k + 1, ITERS):
            s = s - H[k][j] * y[j]
        y[k] = s / H[k][k]

    wide = [jnp.broadcast_to(c, (8, 128))[None] for c in y]
    total = wide[0] * V[0].reshape(32, 8, 128)
    rest = Z[1].reshape(32, 8, 128) - wide[0] * A[0].reshape(32, 8, 128)
    for j in range(1, ITERS):
        total = total + wide[j] * V[j].reshape(32, 8, 128)
        rest = rest - wide[j] * A[j].reshape(32, 8, 128)
    sol_ref[...] = total.reshape(16, 16, 128)
    res_ref[...] = rest.reshape(16, 16, 128)

    sent(0, 2)

    def settle(s, c):
        sent(s, 1)
        return c

    lax.fori_loop(1, ITERS + 1, settle, 0)
    left_a()
    left_b()


def solution(mesh):
    dims = tuple(mesh.shape[a] for a in AXES)
    xwidth = min(4, dims[1] // 2)
    plane, ring = dims[0] * xwidth, dims[1] // xwidth * dims[2]
    near = len(NEAR)
    steps = ITERS + 1
    f32 = jnp.float32
    block = (16, 16, 128)
    vmem = pl.BlockSpec(memory_space=pltpu.VMEM)
    dma = pltpu.SemaphoreType.DMA

    def body(*args):
        def run(*refs):
            kernel(dims, xwidth, *refs)

        mats, facs = constants()
        return pl.pallas_call(
            run,
            out_shape=[jax.ShapeDtypeStruct(block, f32)] * 2,
            in_specs=[vmem] * 7,
            out_specs=[vmem] * 2,
            scratch_shapes=[
                pltpu.VMEM(block, f32),
                pltpu.VMEM((steps, 2) + block, f32),
                pltpu.VMEM(block, f32),
                pltpu.VMEM((ITERS,) + block, f32),
                pltpu.VMEM((ITERS + 1,) + block, f32),
                pltpu.VMEM((ITERS,) + block, f32),
                pltpu.VMEM((steps, 2, 2, 16, 128), f32),
                pltpu.VMEM((steps, 2, 8, 128), f32),
                pltpu.VMEM((steps, 2, 2, 16, 128), f32),
                pltpu.VMEM((steps, 2, 2, 16, 128), f32),
                pltpu.VMEM((steps, 2, 2, 8, 128), f32),
                pltpu.VMEM((steps, 2, 4, 8, 128), f32),
                pltpu.VMEM((steps, 2, 16, 128), f32),
                pltpu.VMEM((24, 8, 128), f32),
                pltpu.VMEM((1, 128), f32),
                pltpu.VMEM((1, 128), f32),
                pltpu.VMEM((plane, 1, 128), f32),
                pltpu.VMEM((ring, 1, 128), f32),
                dma((steps, near)),
                dma((steps, near)),
                dma((plane,)),
                dma((plane,)),
                dma((ring,)),
                dma((ring,)),
            ],
            compiler_params=pltpu.CompilerParams(
                collective_id=0, has_side_effects=True, vmem_limit_bytes=32 * 1024 * 1024
            ),
        )(*args, jnp.asarray(mats), jnp.asarray(facs))

    spec = P(*AXES)
    return jax.shard_map(
        body, mesh=mesh, in_specs=(spec,) * 5, out_specs=(spec,) * 2, check_vma=False
    )
```

time: 890 us -> 98.8 us (0.11)
  blocking collectives: 705 us -> 0 us
  starting transfers between devices: 114 us -> 0 us
  Pallas kernels: 0 us -> 90.3 us
  between operations: 15.6 us -> 0.65 us
  matrix products: 14.8 us -> 0 us
  waiting for transfers between devices: 13.3 us -> 0 us
  other arithmetic: 11.2 us -> 0 us
    psum x4 -> x0, blocking collectives: 705 us -> none  [shards(): lax.psum((jnp.sum(weights * residual * smoothed), jnp.sum(weights * image...]
    ppermute x36 -> x0, starting transfers between devices: 114 us -> none  [the longest x18 66.6 us: with_halo(): lax.ppermute(tail, axis, [(i, (i + 1) % count) for i in range(ends)])]
    pallas_call x0 -> x1, Pallas kernels: none -> 90.3 us  [body(): pl.pallas_call(run, out_shape=[jax.ShapeDtypeStruct(block, f32)] * 2, in_...]
    dot_general x27 -> x0, matrix products: 14.8 us -> none  [the longest x9 9.01 us: apply_along(): jnp.einsum('ki,abci->abck', matrix, blocks, precision=lax.Precision.HIGHEST)]
    ppermute x36 -> x0, waiting for transfers between devices: 13.3 us -> none  [the longest x18 7.44 us: with_halo(): lax.ppermute(tail, axis, [(i, (i + 1) % count) for i in range(ends)])]
  transfers between devices with their start and end apart: 36 -> 0, of which waited for: 12 -> 0; matrix products, arithmetic and copies ran while one was open for 0% -> 0% of each run, Pallas kernels for 0% -> 0%
where the time goes in v1:
time: 98.8 us; the launch traced here: 98.6 us
  Pallas kernels  90.3 us (91%)
  local copies, waits for them, and re-layouts  7.65 us (8%)
    pallas_call x1, Pallas kernels, body(): pl.pallas_call(run, out_shape=[jax.ShapeDtypeStruct(block, f32)] * 2, in_...  90.3 us
    unnamed x16, local copies, waits for them, and re-layouts  7.65 us

profile of v1, /device:TPU:1, one launch (start us, length us, event | category | flops | bytes accessed | tf_op | source)
XLA Modules:
  0.0 98.6 jit_solution(6838032836501531436)
XLA Ops:
  0.6 0.0 copy-start
  0.6 0.9 copy-done
  1.6 0.0 copy-start.1
  1.6 0.9 copy-done.1
  2.5 0.0 copy-start.2
  2.5 0.9 copy-done.2
  3.4 0.0 copy-start.3
  3.4 0.9 copy-done.3
  4.3 0.0 copy-start.4
  4.3 0.9 copy-done.4
  5.2 0.0 copy-start.5
  5.2 0.9 copy-done.5
  6.1 0.0 copy-start.6
  6.1 0.9 copy-done.6
  7.0 90.3 %shard_map.86 = (f32[16,16,128]{2,1,0:T(8,128)S(1)}, f32[16,16,128]{2,1,0:T(8,128)S(1)}) custom-call(f32[16,16,128]{2,1,0:T(8,128)S(1)} %copy-done.1, f32[16,16,128]{2,1,0:T(8,128)S(1)} %copy-done.2, f32[16,16,128]{2,1,0:T(8,128)S(1)} %copy-done.3, f32[16,16,128]{2,1,0:T(8,128)S(1)} %copy-done.4, f32[16,16,128]{2,1,0:T(8,128)S(1)} %copy-done.5, ...), custom_call_target="tpu_custom_call" | custom-call | tf_op jit(solution)/shard_map/pallas_call | solution.py:406
  97.2 0.7 copy.11
  97.9 0.7 copy.12
Async XLA Ops:
  0.6 0.9 copy-start
  1.6 0.9 copy-start.1
  2.5 0.9 copy-start.2
  3.4 0.9 copy-start.3
  4.3 0.9 copy-start.4
  5.2 0.9 copy-start.5
  6.1 0.9 copy-start.6

commit v2 on v1

--- a/solution.py
+++ b/solution.py
@@ -92,10 +92,11 @@
 
 def kernel(
     dims, xwidth,
+    src_hbm, mx_hbm, my_hbm, mz_hbm, mass_hbm, mats_hbm, facs_hbm,
+    sol_ref, res_ref,
     src_ref, mx_ref, my_ref, mz_ref, mass_ref, mats_ref, facs_ref,
-    sol_ref, res_ref,
-    jac, T, L, V, Z, A, YS, PS, XF, YF, ZF, XZ, RB, acc, row_a, row_b, buf_a, buf_b,
-    ssem, rsem, ssem_a, rsem_a, ssem_b, rsem_b,
+    jac, T, L, V, Z, A, YS, PS, XF, YF, ZF, XZ, RB, acc, count, row_a, row_b, buf_a, buf_b,
+    ssem, rsem, ssem_a, rsem_a, ssem_b, rsem_b, lsem,
 ):
     nx, ny, nz = dims
     ix, iy, iz = (lax.axis_index(a) for a in AXES)
@@ -114,30 +115,49 @@
 
     depth = ny // xwidth
     plane, ring = nx * xwidth, depth * nz
-    my_a = ix * xwidth + lax.rem(iy, xwidth)
-    my_b = (iy // xwidth) * nz + iz
+    col, high = lax.rem(iy, xwidth), iy // xwidth
+    my_a = ix * xwidth + col
+    my_b = high * nz + iz
+
+    def carry(at, by, n):
+        to = at + by
+        over = to >= n
+        return jnp.where(over, to - n, to), over.astype(jnp.int32)
 
     def dev_a(k):
-        to = lax.rem(my_a + k, plane)
-        return (to // xwidth, (iy // xwidth) * xwidth + lax.rem(to, xwidth), iz)
+        x, up = carry(col, k % xwidth, xwidth)
+        return carry(ix, k // xwidth + up, nx)[0], high * xwidth + x, iz
 
     def dev_b(k):
-        to = lax.rem(my_b + k, ring)
-        return (ix, (to // nz) * xwidth + lax.rem(iy, xwidth), lax.rem(to, nz))
-
-    def far_first(i, n):
-        half = (i + 1) // 2
-        return n // 2 + jnp.where(lax.rem(i, 2) == 1, half, -half)
-
+        z, up = carry(iz, k % nz, nz)
+        return ix, carry(high, k // nz + up, depth)[0] * xwidth + col, z
+
+    def far_first(n):
+        return sorted(range(1, n), key=lambda k: abs(2 * k - n))
+
+    loads = [
+        pltpu.make_async_copy(a, b, lsem.at[i])
+        for i, (a, b) in enumerate(
+            (
+                (src_hbm, src_ref),
+                (mats_hbm, mats_ref),
+                (facs_hbm, facs_ref),
+                (mx_hbm, mx_ref),
+                (my_hbm, my_ref),
+                (mz_hbm, mz_ref),
+                (mass_hbm, mass_ref),
+            )
+        )
+    ]
+    for load in loads:
+        load.start()
     for ref in (XF, YF, ZF, XZ, RB):
-        ref[...] = jnp.zeros_like(ref)
+        ref[0] = jnp.zeros(ref.shape[1:], jnp.float32)
     barrier = pltpu.get_barrier_semaphore()
 
     def greet(group, n):
-        def body(i, c):
-            pl.semaphore_signal(barrier, inc=1, device_id=group(far_first(i, n)), device_id_type=MESH)
-            return c
-        lax.fori_loop(0, n - 1, body, 0)
+        for k in far_first(n):
+            pl.semaphore_signal(barrier, inc=1, device_id=group(k), device_id_type=MESH)
 
     greet(dev_b, ring)
     for o in NEAR:
@@ -182,7 +202,7 @@
 
     def copies(s, fields):
         fs = pl.ds(0, fields)
-        for n, o in enumerate(NEAR):
+        for o in NEAR:
             dx, dy, dz = o
             ex, ey, ez = end(-dx), end(-dy), end(-dz)
             edge = pl.ds(7 * end(dy), 1)
@@ -202,7 +222,7 @@
                 slot = 4 + 2 * ey + ez if dx == 0 else 8 + 4 * ex + 2 * ey + ez
                 dst = RB.at[s, fs, pl.ds(slot, 1)]
             yield o, pltpu.make_async_remote_copy(
-                src_ref=src, dst_ref=dst, send_sem=ssem.at[s, n], recv_sem=rsem.at[s, n],
+                src_ref=src, dst_ref=dst, send_sem=ssem.at[s], recv_sem=rsem.at[s],
                 device_id=dev(o), device_id_type=MESH,
             )
 
@@ -210,15 +230,21 @@
         for o, copy in copies(s, fields):
             pl.when(exists(o))(copy.start)
 
+    def wait_all(sem, fields):
+        for cx, cy, cz in itertools.product((1, 2), repeat=3):
+            rows = 16 * (cx + cy) + 8 * cz + cx * cy + 8 * cx * cz + cy * cz * (1 + cx)
+            here = (sides[0] == cx + 1) & (sides[1] == cy + 1) & (sides[2] == cz + 1)
+
+            @pl.when(here)
+            def _(rows=rows):
+                whole = count.at[pl.ds(0, rows * fields)]
+                pltpu.make_async_copy(whole, whole, sem).wait()
+
     def receive(s, fields):
-        order = {o: n for n, o in enumerate(NEAR)}
-        for o, copy in copies(s, fields):
-            back = tuple(-d for d in o)
-            pl.when(exists(back))(copy.wait_recv)
+        wait_all(rsem.at[s], fields)
 
     def sent(s, fields):
-        for o, copy in copies(s, fields):
-            pl.when(exists(o))(copy.wait_send)
+        wait_all(ssem.at[s], fields)
 
     def merge(minus, plus):
         return jnp.where(even, pltpu.roll(plus, 127, 1), pltpu.roll(minus, 1, 1))
@@ -266,21 +292,26 @@
     def product(slot, a, b):
         acc[slot] = jnp.sum((a * b).reshape(32, 8, 128), axis=0)
 
-    def products(j, count):
-        for i in range(count):
+    def products(j, upto):
+        for i in range(upto):
             product(4 * j + i, L[...], V[i])
         product(16 + j, src_ref[...], V[j])
 
+    for ref in (XF, YF, ZF, XZ, RB):
+        ref[1:] = jnp.zeros((ITERS,) + ref.shape[1:], jnp.float32)
+    V[...] = jnp.zeros_like(V)
+    acc[...] = jnp.zeros_like(acc)
+    Z[0] = jnp.zeros((16, 16, 128), jnp.float32)
+    loads[0].wait()
+    prepare(0, 0, src_ref[...])
+    for load in loads[1:]:
+        load.wait()
     diag = mass_ref[...] + jnp.stack(along_x_plain(slabs(mx_ref[...]), (TABLE * TABLE).T))
     diag = diag + along_y(my_ref[...].reshape(32, 8, 128), facs_ref[2]).reshape(16, 16, 128)
     diag = diag + along_z(mz_ref[...], mats_ref[2]).reshape(16, 16, 128)
-    prepare(0, 0, src_ref[...])
     prepare(0, 1, diag)
     pl.semaphore_wait(barrier, n_near + (plane - 1) + (ring - 1))
     send(0, 2)
-    V[...] = jnp.zeros_like(V)
-    acc[...] = jnp.zeros_like(acc)
-    Z[0] = jnp.zeros((16, 16, 128), jnp.float32)
     receive(0, 2)
     finish(0, 0, Z.at[1])
     finish(0, 1, jac)
@@ -314,27 +345,13 @@
         row[...] = values
         buf[me] = values
 
-        def copy(i):
-            k = far_first(i, n)
-            return pltpu.make_async_remote_copy(
-                src_ref=row, dst_ref=buf.at[me], send_sem=ss.at[k], recv_sem=rs.at[k],
+        for k in far_first(n):
+            pltpu.make_async_remote_copy(
+                src_ref=row, dst_ref=buf.at[me], send_sem=ss, recv_sem=rs,
                 device_id=group(k), device_id_type=MESH,
-            )
-
-        def begin(i, c):
-            copy(i).start()
-            return c
-
-        def arrive(i, c):
-            copy(i).wait_recv()
-            return c
-
-        def left(i, c):
-            copy(i).wait_send()
-            return c
-
-        lax.fori_loop(0, n - 1, begin, 0)
-        return lambda: lax.fori_loop(0, n - 1, arrive, 0), lambda: lax.fori_loop(0, n - 1, left, 0)
+            ).start()
+        peers = buf.at[pl.ds(0, n - 1)]
+        return lambda: pltpu.make_async_copy(peers, peers, rs).wait(), lambda: pltpu.make_async_copy(peers, peers, ss).wait()
 
     values = jnp.sum(jnp.where(pick, sums, 0.0), axis=0, keepdims=True)
     arrive_a, left_a = share(row_a, buf_a, my_a, dev_a, plane, ssem_a, rsem_a, values)
@@ -391,7 +408,6 @@
     dims = tuple(mesh.shape[a] for a in AXES)
     xwidth = min(4, dims[1] // 2)
     plane, ring = dims[0] * xwidth, dims[1] // xwidth * dims[2]
-    near = len(NEAR)
     steps = ITERS + 1
     f32 = jnp.float32
     block = (16, 16, 128)
@@ -405,10 +421,13 @@
         mats, facs = constants()
         return pl.pallas_call(
             run,
-            out_shape=[jax.ShapeDtypeStruct(block, f32)] * 2,
-            in_specs=[vmem] * 7,
+            out_shape=[pltpu.VMEM(block, f32)] * 2,
+            in_specs=[pl.BlockSpec(memory_space=pltpu.HBM)] * 7,
             out_specs=[vmem] * 2,
             scratch_shapes=[
+                *[pltpu.VMEM(block, f32)] * 5,
+                pltpu.VMEM(mats.shape, f32),
+                pltpu.VMEM(facs.shape, f32),
                 pltpu.VMEM(block, f32),
                 pltpu.VMEM((steps, 2) + block, f32),
                 pltpu.VMEM(block, f32),
@@ -423,21 +442,23 @@
                 pltpu.VMEM((steps, 2, 4, 8, 128), f32),
                 pltpu.VMEM((steps, 2, 16, 128), f32),
                 pltpu.VMEM((24, 8, 128), f32),
+                pltpu.VMEM((256, 128), f32),
                 pltpu.VMEM((1, 128), f32),
                 pltpu.VMEM((1, 128), f32),
                 pltpu.VMEM((plane, 1, 128), f32),
                 pltpu.VMEM((ring, 1, 128), f32),
-                dma((steps, near)),
-                dma((steps, near)),
-                dma((plane,)),
-                dma((plane,)),
-                dma((ring,)),
-                dma((ring,)),
+                dma((steps,)),
+                dma((steps,)),
+                dma,
+                dma,
+                dma,
+                dma,
+                dma((7,)),
             ],
             compiler_params=pltpu.CompilerParams(
                 collective_id=0, has_side_effects=True, vmem_limit_bytes=32 * 1024 * 1024
             ),
-        )(*args, jnp.asarray(mats), jnp.asarray(facs))
+        )(*(pltpu.with_memory_space_constraint(a, pltpu.HBM) for a in (*args, jnp.asarray(mats), jnp.asarray(facs))))
 
     spec = P(*AXES)
     return jax.shard_map(

time: 98.8 us -> 88.2 us (0.89)
  local copies, waits for them, and re-layouts: 7.65 us -> 1.31 us
  Pallas kernels: 90.3 us -> 86.1 us
    unnamed x16 -> x2, local copies, waits for them, and re-layouts: 7.65 us -> 1.31 us
    pallas_call x1, Pallas kernels: 90.3 us -> 86.1 us  [body(): pl.pallas_call(run, out_shape=[pltpu.VMEM(block, f32)] * 2, in_specs=[pl....]
where the time goes in v2:
time: 88.2 us; the launch traced here: 88 us
  Pallas kernels  86.1 us (98%)
  local copies, waits for them, and re-layouts  1.31 us (1%)
    pallas_call x1, Pallas kernels, body(): pl.pallas_call(run, out_shape=[pltpu.VMEM(block, f32)] * 2, in_specs=[pl....  86.1 us

profile of v2, /device:TPU:1, one launch (start us, length us, event | category | flops | bytes accessed | tf_op | source)
XLA Modules:
  0.0 88.0 jit_solution(989920436320340299)
XLA Ops:
  0.6 86.1 %shard_map.86 = (f32[16,16,128]{2,1,0:T(8,128)S(1)}, f32[16,16,128]{2,1,0:T(8,128)S(1)}) custom-call(f32[16,16,128]{2,1,0:T(8,128)} %refs_0_.1, f32[16,16,128]{2,1,0:T(8,128)} %refs_1_.1, f32[16,16,128]{2,1,0:T(8,128)} %refs_2_.1, f32[16,16,128]{2,1,0:T(8,128)} %refs_3_.1, f32[16,16,128]{2,1,0:T(8,128)} %refs_4_.1, f32[3,128,128]{2,1,0:T(8,128)} %constant.4.clone.refs_5_, ...), custom_call_target="tpu_custom_call" | custom-call | tf_op jit(solution)/shard_map/pallas_call | solution.py:422
  86.7 0.7 copy.11
  87.4 0.7 copy.12

commit v3 on v2

--- a/solution.py
+++ b/solution.py
@@ -82,7 +82,7 @@
 
 
 def along_z(field, mat):
-    flat = field.reshape(256, 128)
+    flat = field.reshape(-1, 128)
     return jnp.dot(flat, mat, precision=lax.Precision.HIGHEST, preferred_element_type=jnp.float32)
 
 
@@ -95,7 +95,7 @@
     src_hbm, mx_hbm, my_hbm, mz_hbm, mass_hbm, mats_hbm, facs_hbm,
     sol_ref, res_ref,
     src_ref, mx_ref, my_ref, mz_ref, mass_ref, mats_ref, facs_ref,
-    jac, T, L, V, Z, A, YS, PS, XF, YF, ZF, XZ, RB, acc, count, row_a, row_b, buf_a, buf_b,
+    jac, T, L, V, Z, A, YS, PS, PR, FC, XF, YF, ZF, XZ, RB, acc, count, row_a, row_b, buf_a, buf_b,
     ssem, rsem, ssem_a, rsem_a, ssem_b, rsem_b, lsem,
 ):
     nx, ny, nz = dims
@@ -169,18 +169,28 @@
     n_near = sides[0] * sides[1] * sides[2] - 1
 
     lane = lax.broadcasted_iota(jnp.int32, (8, 128), 1)
-    sub = lax.broadcasted_iota(jnp.int32, (8, 128), 0)
     within = lax.rem(lane, 8)
     close = jnp.where((within == 7) & (lane != 127), 1.0, 0.0)[None]
     opens = jnp.where((within == 0) & (lane != 0), 1.0, 0.0)[None]
     even = lax.rem(lane, 2) == 0
-    low = lax.rem(lane, 4) < 2
-    ends_y = (low & (sub == 0)) | (jnp.logical_not(low) & (sub == 7))
     ends_z = (lane == 0) | (lane == 127)
 
-    def prepare(s, f, raw):
+    lane16 = lax.broadcasted_iota(jnp.int32, (16, 128), 1)
+    row16 = lax.broadcasted_iota(jnp.int32, (16, 128), 0)
+
+    def rows(ref):
+        return ref[:, 0, :], ref[:, 15, :]
+
+    def add_rows(ref, parts):
+        ref[:, 0, :] = ref[:, 0, :] + parts[0]
+        ref[:, 15, :] = ref[:, 15, :] + parts[1]
+
+    def inside(v):
+        return v + pltpu.roll(v, 127, 2) * close + pltpu.roll(v, 1, 2) * opens
+
+    def prepare(s, f, raw, faces):
         v = raw.reshape(32, 8, 128)
-        v = v + pltpu.roll(v, 127, 2) * close + pltpu.roll(v, 1, 2) * opens
+        v = inside(v)
         t = T.at[s, f]
         t[...] = v.reshape(16, 16, 128)
         both = t[7] + t[8]
@@ -189,23 +199,41 @@
         both = t[:, 7, :] + t[:, 8, :]
         t[:, 7, :] = both
         t[:, 8, :] = both
-        YS[s, f, 0] = t[:, 0, :]
-        YS[s, f, 1] = t[:, 15, :]
+        if faces:
+            YS[s, f, 0], YS[s, f, 1] = rows(t)
         packed = jnp.zeros((8, 128), jnp.float32)
         for i in range(32):
             tile = t[i // 2, pl.ds(8 * (i % 2), 8), :]
             packed = jnp.where(lane // 2 == i, pltpu.roll(tile, 2 * i + 1, 1), packed)
         PS[s, f] = packed
+        if faces:
+            PR[s, f, pl.ds(0, 1)] = packed[0:1]
+            PR[s, f, pl.ds(1, 1)] = packed[7:8]
+
+    def prepare_faces(s, parts):
+        v = inside(jnp.concatenate(parts, axis=0).reshape(4, 8, 128))
+        ys = YS.at[s, 0]
+        ys[...] = v.reshape(2, 16, 128)
+        for e in (0, 1):
+            both = ys[e, pl.ds(7, 1), :] + ys[e, pl.ds(8, 1), :]
+            ys[e, pl.ds(7, 1), :] = both
+            ys[e, pl.ds(8, 1), :] = both
+            face = ys[e]
+            to = 4 * row16 + 2 * e
+            line = jnp.where(lane16 == to, face[:, 127:128], 0.0)
+            line = jnp.where(lane16 == to + 1, face[:, 0:1], line)
+            PR[s, 0, pl.ds(e, 1)] = jnp.sum(line, axis=0, keepdims=True)
 
     def end(d):
         return 0 if d < 0 else 1
 
-    def copies(s, fields):
+    def copies(s, fields, far):
         fs = pl.ds(0, fields)
         for o in NEAR:
             dx, dy, dz = o
+            if (dy != 0) != far:
+                continue
             ex, ey, ez = end(-dx), end(-dy), end(-dz)
-            edge = pl.ds(7 * end(dy), 1)
             if dz == 0:
                 if dy == 0:
                     src, dst = T.at[s, fs, 15 * end(dx)], XF.at[s, fs, ex]
@@ -218,74 +246,98 @@
                 src = PS.at[s, fs]
                 dst = ZF.at[s, fs, ez] if dx == 0 else XZ.at[s, fs, 2 * ex + ez]
             else:
-                src = PS.at[s, fs, edge]
+                src = PR.at[s, fs, pl.ds(end(dy), 1)]
                 slot = 4 + 2 * ey + ez if dx == 0 else 8 + 4 * ex + 2 * ey + ez
                 dst = RB.at[s, fs, pl.ds(slot, 1)]
             yield o, pltpu.make_async_remote_copy(
-                src_ref=src, dst_ref=dst, send_sem=ssem.at[s], recv_sem=rsem.at[s],
+                src_ref=src, dst_ref=dst, send_sem=ssem.at[s, int(far)], recv_sem=rsem.at[s, int(far)],
                 device_id=dev(o), device_id_type=MESH,
             )
 
-    def send(s, fields):
-        for o, copy in copies(s, fields):
+    def send(s, fields, far):
+        for o, copy in copies(s, fields, far):
             pl.when(exists(o))(copy.start)
 
-    def wait_all(sem, fields):
-        for cx, cy, cz in itertools.product((1, 2), repeat=3):
-            rows = 16 * (cx + cy) + 8 * cz + cx * cy + 8 * cx * cz + cy * cz * (1 + cx)
-            here = (sides[0] == cx + 1) & (sides[1] == cy + 1) & (sides[2] == cz + 1)
-
-            @pl.when(here)
-            def _(rows=rows):
-                whole = count.at[pl.ds(0, rows * fields)]
+    def wait_all(sem, fields, far):
+        for cx, cy, cz in itertools.product((1, 2), (1, 2) if far else (0,), (1, 2)):
+            if far:
+                total = 16 * cy + cx * cy + cy * cz * (1 + cx)
+            else:
+                total = 16 * cx + 8 * cz + 8 * cx * cz
+            match = (sides[0] == cx + 1) & (sides[2] == cz + 1)
+            if far:
+                match = match & (sides[1] == cy + 1)
+
+            @pl.when(match)
+            def _(total=total):
+                whole = count.at[pl.ds(0, total * fields)]
                 pltpu.make_async_copy(whole, whole, sem).wait()
 
-    def receive(s, fields):
-        wait_all(rsem.at[s], fields)
+    def receive(s, fields, far):
+        wait_all(rsem.at[s, int(far)], fields, far)
 
     def sent(s, fields):
-        wait_all(ssem.at[s], fields)
+        for far in (True, False):
+            wait_all(ssem.at[s, int(far)], fields, far)
 
     def merge(minus, plus):
         return jnp.where(even, pltpu.roll(plus, 127, 1), pltpu.roll(minus, 1, 1))
 
-    def finish(s, f, out):
-        rb = RB.at[s, f]
-
-        def line(k):
-            return jnp.broadcast_to(rb[pl.ds(k, 1), :], (8, 128))
-
-        def with_y(m, first):
-            minus = merge(line(first), line(first + 1))
-            plus = merge(line(first + 2), line(first + 3))
-            c = jnp.where(low, pltpu.roll(minus, 126, 1), pltpu.roll(plus, 2, 1))
-            return m + jnp.where(ends_y, c, 0.0)
-
-        m = with_y(merge(ZF[s, f, 0], ZF[s, f, 1]), 4)
-        m_minus = with_y(merge(XZ[s, f, 0], XZ[s, f, 1]), 8)
-        m_plus = with_y(merge(XZ[s, f, 2], XZ[s, f, 3]), 12)
-        m = m + jnp.where(lane < 4, pltpu.roll(m_minus, 68, 1), 0.0)
-        m = m + jnp.where((lane >= 60) & (lane < 64), pltpu.roll(m_plus, 60, 1), 0.0)
+    def shifted(m, minus, plus):
+        m = m + jnp.where(lane < 4, pltpu.roll(minus, 68, 1), 0.0)
+        return m + jnp.where((lane >= 60) & (lane < 64), pltpu.roll(plus, 60, 1), 0.0)
+
+    def finish_near(s, f, out):
+        m = merge(ZF[s, f, 0], ZF[s, f, 1])
+        m = shifted(m, merge(XZ[s, f, 0], XZ[s, f, 1]), merge(XZ[s, f, 2], XZ[s, f, 3]))
         for i in range(32):
             at = (i // 2, pl.ds(8 * (i % 2), 8), slice(None))
             part = jnp.where(ends_z, pltpu.roll(m, 127 - 2 * i, 1), 0.0)
             out[at] = T[(s, f) + at] + part
-        out[:, 0, :] = out[:, 0, :] + YF[s, f, 0]
-        out[:, 15, :] = out[:, 15, :] + YF[s, f, 1]
         for e in (0, 1):
             out[15 * e] = out[15 * e] + XF[s, f, e]
-            for g in (0, 1):
-                r = pl.ds(15 * g, 1)
-                out[15 * e, r, :] = out[15 * e, r, :] + rb[pl.ds(2 * e + g, 1), :]
+
+    def from_far(s, f):
+        rb = RB.at[s, f]
+
+        def line(k):
+            return jnp.broadcast_to(rb[pl.ds(k, 1), :], (8, 128))
+
+        parts = []
+        for e in (0, 1):
+            m, minus, plus = (merge(line(k + 2 * e), line(k + 2 * e + 1)) for k in (4, 8, 12))
+            m = jnp.broadcast_to(shifted(m, minus, plus)[0:1], (16, 128))
+            at = 4 * row16 + 2 * (1 - e)
+            last = jnp.sum(jnp.where(lane16 == at, m, 0.0), axis=1, keepdims=True)
+            first = jnp.sum(jnp.where(lane16 == at + 1, m, 0.0), axis=1, keepdims=True)
+            part = YF[s, f, e]
+            part = part + jnp.where(row16 == 0, rb[pl.ds(e, 1), :], 0.0)
+            part = part + jnp.where(row16 == 15, rb[pl.ds(2 + e, 1), :], 0.0)
+            part = part + jnp.where(lane16 == 0, first, 0.0) + jnp.where(lane16 == 127, last, 0.0)
+            parts.append(part)
+        return parts
+
+    def finish(s, f, out):
+        finish_near(s, f, out)
+        add_rows(out, from_far(s, f))
+
+    def local_y(v):
+        v3 = v.reshape(32, 8, 128)
+        slope = my_ref[...].reshape(32, 8, 128) * along_y(v3, facs_ref[0])
+        return mass_ref[...] * v + along_y(slope, facs_ref[1]).reshape(16, 16, 128)
+
+    def local_faces(parts, gains):
+        flat = jnp.concatenate(parts, axis=0)
+        slope = gains[0].reshape(4, 8, 128) * along_y(flat.reshape(4, 8, 128), facs_ref[0])
+        total = along_y(slope, facs_ref[1]).reshape(32, 128)
+        total = total + along_z(gains[1] * along_z(flat, mats_ref[0]), mats_ref[1])
+        return total[:16], total[16:]
 
     def local(v):
-        total = mass_ref[...] * v
+        total = local_y(v)
         slope = along_x(slabs(v), TABLE)
         slope = [mx_ref[i] * slope[i] for i in range(16)]
         total = total + jnp.stack(along_x(slope, TABLE.T))
-        v3 = v.reshape(32, 8, 128)
-        slope = my_ref[...].reshape(32, 8, 128) * along_y(v3, facs_ref[0])
-        total = total + along_y(slope, facs_ref[1]).reshape(16, 16, 128)
         slope = mz_ref[...].reshape(256, 128) * along_z(v, mats_ref[0])
         return total + along_z(slope, mats_ref[1]).reshape(16, 16, 128)
 
@@ -303,36 +355,57 @@
     acc[...] = jnp.zeros_like(acc)
     Z[0] = jnp.zeros((16, 16, 128), jnp.float32)
     loads[0].wait()
-    prepare(0, 0, src_ref[...])
+    prepare(0, 0, src_ref[...], True)
     for load in loads[1:]:
         load.wait()
     diag = mass_ref[...] + jnp.stack(along_x_plain(slabs(mx_ref[...]), (TABLE * TABLE).T))
-    diag = diag + along_y(my_ref[...].reshape(32, 8, 128), facs_ref[2]).reshape(16, 16, 128)
+    L[...] = along_y(my_ref[...].reshape(32, 8, 128), facs_ref[2]).reshape(16, 16, 128)
+    diag = diag + L[...]
     diag = diag + along_z(mz_ref[...], mats_ref[2]).reshape(16, 16, 128)
-    prepare(0, 1, diag)
+    prepare(0, 1, diag, True)
     pl.semaphore_wait(barrier, n_near + (plane - 1) + (ring - 1))
-    send(0, 2)
-    receive(0, 2)
+    send(0, 2, True)
+    send(0, 2, False)
+    both = [jnp.concatenate(rows(ref), axis=0) for ref in (mx_ref, mz_ref)]
+    FC[0], FC[1] = both
+    FC[2] = jnp.concatenate([a + b for a, b in zip(rows(mass_ref), rows(L))], axis=0)
+    receive(0, 2, False)
+    receive(0, 2, True)
     finish(0, 0, Z.at[1])
     finish(0, 1, jac)
     jac[...] = 1.0 / jac[...]
     V[0] = jac[...] * Z[1]
-
-    def step(j, c):
+    L[...] = local_y(V[0])
+    more = local_faces(rows(V.at[0]), (FC[0], FC[1]))
+    prepare_faces(1, [a + b for a, b in zip(rows(L), more)])
+    send(1, 1, True)
+
+    for j in range(ITERS - 1):
+        s = j + 1
         L[...] = local(V[j])
-        prepare(j + 1, 0, L[...])
-        send(j + 1, 1)
+        prepare(s, 0, L[...], False)
+        send(s, 1, False)
         products(j, ITERS)
-        receive(j + 1, 1)
-        finish(j + 1, 0, A.at[j])
-        first = j == 0
-        gain = jnp.where(first, 1.0 / HALF, 2.0 / HALF)
-        z = gain * (A[j] - CENTRE * Z[j + 1]) - jnp.where(first, 0.0, 1.0) * Z[j]
+        receive(s, 1, False)
+        finish_near(s, 0, A.at[j])
+        gain = (1.0 if j == 0 else 2.0) / HALF
+        z = gain * (A[j] - CENTRE * Z[j + 1]) - (0.0 if j == 0 else 1.0) * Z[j]
         Z[j + 2] = z
         V[j + 1] = jac[...] * z
-        return c
-
-    lax.fori_loop(0, ITERS - 1, step, 0)
+        if j < ITERS - 2:
+            L[...] = local_y(V[j + 1])
+        receive(s, 1, True)
+        d_image = from_far(s, 0)
+        d_base = [gain * d for d in d_image]
+        d_smooth = [a * b for a, b in zip(rows(jac), d_base)]
+        if j < ITERS - 2:
+            more = local_faces([a + b for a, b in zip(rows(V.at[j + 1]), d_smooth)], (FC[0], FC[1]))
+            own = [FC[2, pl.ds(16 * e, 16)] * d_smooth[e] for e in (0, 1)]
+            prepare_faces(s + 1, [a + b + c for a, b, c in zip(rows(L), more, own)])
+            send(s + 1, 1, True)
+        add_rows(A.at[j], d_image)
+        add_rows(Z.at[j + 2], d_base)
+        add_rows(V.at[j + 1], d_smooth)
 
     last = ITERS - 1
     L[...] = local(V[last])
@@ -355,13 +428,23 @@
 
     values = jnp.sum(jnp.where(pick, sums, 0.0), axis=0, keepdims=True)
     arrive_a, left_a = share(row_a, buf_a, my_a, dev_a, plane, ssem_a, rsem_a, values)
-    prepare(ITERS, 0, L[...])
-    send(ITERS, 1)
+    prepare(ITERS, 0, L[...], True)
+    send(ITERS, 1, True)
+    send(ITERS, 1, False)
     arrive_a()
     values = jnp.sum(buf_a[...], axis=0)
     arrive_b, left_b = share(row_b, buf_b, my_b, dev_b, ring, ssem_b, rsem_b, values)
-    receive(ITERS, 1)
+    receive(ITERS, 1, False)
+    receive(ITERS, 1, True)
     finish(ITERS, 0, A.at[last])
+    sent(0, 2)
+
+    def settle(s, c):
+        sent(s, 1)
+        return c
+
+    lax.fori_loop(1, ITERS + 1, settle, 0)
+    left_a()
     arrive_b()
     values = jnp.broadcast_to(jnp.sum(buf_b[...], axis=0), (8, 128))
 
@@ -393,14 +476,6 @@
     sol_ref[...] = total.reshape(16, 16, 128)
     res_ref[...] = rest.reshape(16, 16, 128)
 
-    sent(0, 2)
-
-    def settle(s, c):
-        sent(s, 1)
-        return c
-
-    lax.fori_loop(1, ITERS + 1, settle, 0)
-    left_a()
     left_b()
 
 
@@ -436,6 +511,8 @@
                 pltpu.VMEM((ITERS,) + block, f32),
                 pltpu.VMEM((steps, 2, 2, 16, 128), f32),
                 pltpu.VMEM((steps, 2, 8, 128), f32),
+                pltpu.VMEM((steps, 2, 8, 128), f32),
+                pltpu.VMEM((3, 32, 128), f32),
                 pltpu.VMEM((steps, 2, 2, 16, 128), f32),
                 pltpu.VMEM((steps, 2, 2, 16, 128), f32),
                 pltpu.VMEM((steps, 2, 2, 8, 128), f32),
@@ -447,8 +524,8 @@
                 pltpu.VMEM((1, 128), f32),
                 pltpu.VMEM((plane, 1, 128), f32),
                 pltpu.VMEM((ring, 1, 128), f32),
-                dma((steps,)),
-                dma((steps,)),
+                dma((steps, 2)),
+                dma((steps, 2)),
                 dma,
                 dma,
                 dma,

time: 88.2 us -> 85.9 us (0.974)
  Pallas kernels: 86.1 us -> 83.8 us
    pallas_call x1, Pallas kernels: 86.1 us -> 83.8 us  [body(): pl.pallas_call(run, out_shape=[pltpu.VMEM(block, f32)] * 2, in_specs=[pl....]
where the time goes in v3:
time: 85.9 us; the launch traced here: 85.7 us
  Pallas kernels  83.8 us (98%)
  local copies, waits for them, and re-layouts  1.31 us (2%)
    pallas_call x1, Pallas kernels, body(): pl.pallas_call(run, out_shape=[pltpu.VMEM(block, f32)] * 2, in_specs=[pl....  83.8 us

profile of v3, /device:TPU:1, one launch (start us, length us, event | category | flops | bytes accessed | tf_op | source)
XLA Modules:
  0.0 85.7 jit_solution(7915071149219815349)
XLA Ops:
  0.6 83.8 %shard_map.86 = (f32[16,16,128]{2,1,0:T(8,128)S(1)}, f32[16,16,128]{2,1,0:T(8,128)S(1)}) custom-call(f32[16,16,128]{2,1,0:T(8,128)} %refs_0_.1, f32[16,16,128]{2,1,0:T(8,128)} %refs_1_.1, f32[16,16,128]{2,1,0:T(8,128)} %refs_2_.1, f32[16,16,128]{2,1,0:T(8,128)} %refs_3_.1, f32[16,16,128]{2,1,0:T(8,128)} %refs_4_.1, f32[3,128,128]{2,1,0:T(8,128)} %constant.4.clone.refs_5_, ...), custom_call_target="tpu_custom_call" | custom-call | tf_op jit(solution)/shard_map/pallas_call | solution.py:497
  84.4 0.7 copy.11
  85.1 0.7 copy.12

commit v4 on v3

--- a/solution.py
+++ b/solution.py
@@ -48,11 +48,21 @@
     return np.repeat(rows[:, :, None], 128, axis=2)
 
 
+def lane_factors(matrix):
+    k = np.arange(128)
+    rows = np.zeros((16, 128))
+    for s in range(-7, 8):
+        to = k % 8 + s
+        rows[7 + s] = np.where((to >= 0) & (to < 8), matrix[k % 8, np.clip(to, 0, 7)], 0.0)
+    return rows
+
+
 def constants():
     square = (TABLE * TABLE).T
     mats = [np.kron(np.eye(16), m.T) for m in (TABLE, TABLE.T, square)]
     facs = [sublane_factors(m) for m in (TABLE, TABLE.T, square)]
-    return np.stack(mats).astype(np.float32), np.stack(facs).astype(np.float32)
+    lanes = [lane_factors(m) for m in (TABLE, TABLE.T)]
+    return tuple(np.stack(a).astype(np.float32) for a in (mats, facs, lanes))
 
 
 def along_x(field, matrix):
@@ -81,6 +91,16 @@
     return total
 
 
+def along_lanes(field, facs):
+    parts = [field * facs[pl.ds(7, 1), :][None]]
+    for s in range(-7, 8):
+        if s != 0:
+            parts.append(pltpu.roll(field, -s % 128, 2) * facs[pl.ds(7 + s, 1), :][None])
+    while len(parts) > 1:
+        parts = [sum(parts[i : i + 2]) for i in range(0, len(parts), 2)]
+    return parts[0]
+
+
 def along_z(field, mat):
     flat = field.reshape(-1, 128)
     return jnp.dot(flat, mat, precision=lax.Precision.HIGHEST, preferred_element_type=jnp.float32)
@@ -92,10 +112,10 @@
 
 def kernel(
     dims, xwidth,
-    src_hbm, mx_hbm, my_hbm, mz_hbm, mass_hbm, mats_hbm, facs_hbm,
+    src_hbm, mx_hbm, my_hbm, mz_hbm, mass_hbm, mats_hbm, facs_hbm, lanes_hbm,
     sol_ref, res_ref,
-    src_ref, mx_ref, my_ref, mz_ref, mass_ref, mats_ref, facs_ref,
-    jac, T, L, V, Z, A, YS, PS, PR, FC, XF, YF, ZF, XZ, RB, acc, count, row_a, row_b, buf_a, buf_b,
+    src_ref, mx_ref, my_ref, mz_ref, mass_ref, mats_ref, facs_ref, lanes_ref,
+    jac, T, Y, L, V, Z, A, YS, PS, PR, FC, XF, YF, ZF, XZ, RB, acc, count, row_a, row_b, buf_a, buf_b,
     ssem, rsem, ssem_a, rsem_a, ssem_b, rsem_b, lsem,
 ):
     nx, ny, nz = dims
@@ -146,6 +166,7 @@
                 (my_hbm, my_ref),
                 (mz_hbm, mz_ref),
                 (mass_hbm, mass_ref),
+                (lanes_hbm, lanes_ref),
             )
         )
     ]
@@ -184,6 +205,10 @@
     def add_rows(ref, parts):
         ref[:, 0, :] = ref[:, 0, :] + parts[0]
         ref[:, 15, :] = ref[:, 15, :] + parts[1]
+
+    def set_rows(ref, parts):
+        ref[:, 0, :] = parts[0]
+        ref[:, 15, :] = parts[1]
 
     def inside(v):
         return v + pltpu.roll(v, 127, 2) * close + pltpu.roll(v, 1, 2) * opens
@@ -327,10 +352,11 @@
         return mass_ref[...] * v + along_y(slope, facs_ref[1]).reshape(16, 16, 128)
 
     def local_faces(parts, gains):
-        flat = jnp.concatenate(parts, axis=0)
-        slope = gains[0].reshape(4, 8, 128) * along_y(flat.reshape(4, 8, 128), facs_ref[0])
-        total = along_y(slope, facs_ref[1]).reshape(32, 128)
-        total = total + along_z(gains[1] * along_z(flat, mats_ref[0]), mats_ref[1])
+        both = jnp.concatenate(parts, axis=0).reshape(4, 8, 128)
+        slope = gains[1].reshape(4, 8, 128) * along_lanes(both, lanes_ref.at[0])
+        total = along_lanes(slope, lanes_ref.at[1])
+        slope = gains[0].reshape(4, 8, 128) * along_y(both, facs_ref[0])
+        total = (total + along_y(slope, facs_ref[1])).reshape(32, 128)
         return total[:16], total[16:]
 
     def local(v):
@@ -344,14 +370,8 @@
     def product(slot, a, b):
         acc[slot] = jnp.sum((a * b).reshape(32, 8, 128), axis=0)
 
-    def products(j, upto):
-        for i in range(upto):
-            product(4 * j + i, L[...], V[i])
-        product(16 + j, src_ref[...], V[j])
-
     for ref in (XF, YF, ZF, XZ, RB):
         ref[1:] = jnp.zeros((ITERS,) + ref.shape[1:], jnp.float32)
-    V[...] = jnp.zeros_like(V)
     acc[...] = jnp.zeros_like(acc)
     Z[0] = jnp.zeros((16, 16, 128), jnp.float32)
     loads[0].wait()
@@ -359,8 +379,8 @@
     for load in loads[1:]:
         load.wait()
     diag = mass_ref[...] + jnp.stack(along_x_plain(slabs(mx_ref[...]), (TABLE * TABLE).T))
-    L[...] = along_y(my_ref[...].reshape(32, 8, 128), facs_ref[2]).reshape(16, 16, 128)
-    diag = diag + L[...]
+    Y[...] = along_y(my_ref[...].reshape(32, 8, 128), facs_ref[2]).reshape(16, 16, 128)
+    diag = diag + Y[...]
     diag = diag + along_z(mz_ref[...], mats_ref[2]).reshape(16, 16, 128)
     prepare(0, 1, diag, True)
     pl.semaphore_wait(barrier, n_near + (plane - 1) + (ring - 1))
@@ -368,48 +388,73 @@
     send(0, 2, False)
     both = [jnp.concatenate(rows(ref), axis=0) for ref in (mx_ref, mz_ref)]
     FC[0], FC[1] = both
-    FC[2] = jnp.concatenate([a + b for a, b in zip(rows(mass_ref), rows(L))], axis=0)
+    FC[2] = jnp.concatenate([a + b for a, b in zip(rows(mass_ref), rows(Y))], axis=0)
+    def far_faces(s, smooth, change):
+        more = local_faces(smooth, (FC[0], FC[1]))
+        own = [FC[2, pl.ds(16 * e, 16)] * change[e] for e in (0, 1)]
+        prepare_faces(s, [a + b + c for a, b, c in zip(rows(Y), more, own)])
+        send(s, 1, True)
+
     receive(0, 2, False)
-    receive(0, 2, True)
-    finish(0, 0, Z.at[1])
-    finish(0, 1, jac)
+    finish_near(0, 0, Z.at[1])
+    finish_near(0, 1, jac)
+    diag_rows = rows(jac)
     jac[...] = 1.0 / jac[...]
     V[0] = jac[...] * Z[1]
-    L[...] = local_y(V[0])
-    more = local_faces(rows(V.at[0]), (FC[0], FC[1]))
-    prepare_faces(1, [a + b for a, b in zip(rows(L), more)])
-    send(1, 1, True)
-
-    for j in range(ITERS - 1):
+    Y[...] = local_y(V[0])
+    receive(0, 2, True)
+    d_base = from_far(0, 0)
+    jac_rows = [1.0 / (a + b) for a, b in zip(diag_rows, from_far(0, 1))]
+    smooth = [a * (b + c) for a, b, c in zip(jac_rows, rows(Z.at[1]), d_base)]
+    far_faces(1, smooth, [a - b for a, b in zip(smooth, rows(V.at[0]))])
+    add_rows(Z.at[1], d_base)
+    set_rows(jac, jac_rows)
+    set_rows(V.at[0], smooth)
+
+    last = ITERS - 1
+    for j in range(last):
         s = j + 1
-        L[...] = local(V[j])
-        prepare(s, 0, L[...], False)
+        L[j] = local(V[j])
+        prepare(s, 0, L[j], False)
         send(s, 1, False)
-        products(j, ITERS)
+        for i in range(j + 1):
+            product(4 * j + i, L[j], V[i])
+        product(16 + j, src_ref[...], V[j])
         receive(s, 1, False)
         finish_near(s, 0, A.at[j])
         gain = (1.0 if j == 0 else 2.0) / HALF
         z = gain * (A[j] - CENTRE * Z[j + 1]) - (0.0 if j == 0 else 1.0) * Z[j]
         Z[j + 2] = z
         V[j + 1] = jac[...] * z
-        if j < ITERS - 2:
-            L[...] = local_y(V[j + 1])
+        if j < last - 1:
+            Y[...] = local_y(V[j + 1])
+        else:
+            L[last] = local(V[last])
+            for i in range(ITERS):
+                product(4 * last + i, L[i], V[last])
+            product(16 + last, src_ref[...], V[last])
         receive(s, 1, True)
         d_image = from_far(s, 0)
         d_base = [gain * d for d in d_image]
         d_smooth = [a * b for a, b in zip(rows(jac), d_base)]
-        if j < ITERS - 2:
-            more = local_faces([a + b for a, b in zip(rows(V.at[j + 1]), d_smooth)], (FC[0], FC[1]))
-            own = [FC[2, pl.ds(16 * e, 16)] * d_smooth[e] for e in (0, 1)]
-            prepare_faces(s + 1, [a + b + c for a, b, c in zip(rows(L), more, own)])
-            send(s + 1, 1, True)
+        if j < last - 1:
+            far_faces(s + 1, [a + b for a, b in zip(rows(V.at[j + 1]), d_smooth)], d_smooth)
+        else:
+            more = local_faces(d_smooth, (FC[0], FC[1]))
+            own = [FC[2, pl.ds(16 * e, 16)] * d_smooth[e] + more[e] for e in (0, 1)]
+
+            def add_product(slot, parts):
+                part = sum((a * b).reshape(2, 8, 128)[h] for a, b in zip(parts, d_smooth) for h in (0, 1))
+                acc[slot] = acc[slot] + part
+
+            for i in range(last):
+                add_product(4 * last + i, rows(L.at[i]))
+            add_product(5 * last, [2.0 * a + b for a, b in zip(rows(L.at[last]), own)])
+            add_product(16 + last, rows(src_ref))
         add_rows(A.at[j], d_image)
         add_rows(Z.at[j + 2], d_base)
         add_rows(V.at[j + 1], d_smooth)
 
-    last = ITERS - 1
-    L[...] = local(V[last])
-    products(last, ITERS)
     sums = jnp.sum(acc[...], axis=1)
     sums = jnp.sum(sums, axis=1, keepdims=True)
     pick = lax.broadcasted_iota(jnp.int32, (24, 128), 0) == lax.broadcasted_iota(jnp.int32, (24, 128), 1)
@@ -428,7 +473,7 @@
 
     values = jnp.sum(jnp.where(pick, sums, 0.0), axis=0, keepdims=True)
     arrive_a, left_a = share(row_a, buf_a, my_a, dev_a, plane, ssem_a, rsem_a, values)
-    prepare(ITERS, 0, L[...], True)
+    prepare(ITERS, 0, local(V[last]), True)
     send(ITERS, 1, True)
     send(ITERS, 1, False)
     arrive_a()
@@ -493,19 +538,21 @@
         def run(*refs):
             kernel(dims, xwidth, *refs)
 
-        mats, facs = constants()
+        mats, facs, lanes = constants()
         return pl.pallas_call(
             run,
             out_shape=[pltpu.VMEM(block, f32)] * 2,
-            in_specs=[pl.BlockSpec(memory_space=pltpu.HBM)] * 7,
+            in_specs=[pl.BlockSpec(memory_space=pltpu.HBM)] * 8,
             out_specs=[vmem] * 2,
             scratch_shapes=[
                 *[pltpu.VMEM(block, f32)] * 5,
                 pltpu.VMEM(mats.shape, f32),
                 pltpu.VMEM(facs.shape, f32),
+                pltpu.VMEM(lanes.shape, f32),
                 pltpu.VMEM(block, f32),
                 pltpu.VMEM((steps, 2) + block, f32),
                 pltpu.VMEM(block, f32),
+                pltpu.VMEM((ITERS,) + block, f32),
                 pltpu.VMEM((ITERS,) + block, f32),
                 pltpu.VMEM((ITERS + 1,) + block, f32),
                 pltpu.VMEM((ITERS,) + block, f32),
@@ -530,12 +577,12 @@
                 dma,
                 dma,
                 dma,
-                dma((7,)),
+                dma((8,)),
             ],
             compiler_params=pltpu.CompilerParams(
                 collective_id=0, has_side_effects=True, vmem_limit_bytes=32 * 1024 * 1024
             ),
-        )(*(pltpu.with_memory_space_constraint(a, pltpu.HBM) for a in (*args, jnp.asarray(mats), jnp.asarray(facs))))
+        )(*(pltpu.with_memory_space_constraint(a, pltpu.HBM) for a in (*args, jnp.asarray(mats), jnp.asarray(facs), jnp.asarray(lanes))))
 
     spec = P(*AXES)
     return jax.shard_map(

time: 85.9 us -> 84.4 us (0.983)
  Pallas kernels: 83.8 us -> 82.3 us
    pallas_call x1, Pallas kernels: 83.8 us -> 82.3 us  [body(): pl.pallas_call(run, out_shape=[pltpu.VMEM(block, f32)] * 2, in_specs=[pl....]
where the time goes in v4:
time: 84.4 us; the launch traced here: 84.3 us
  Pallas kernels  82.3 us (98%)
  local copies, waits for them, and re-layouts  1.31 us (2%)
    pallas_call x1, Pallas kernels, body(): pl.pallas_call(run, out_shape=[pltpu.VMEM(block, f32)] * 2, in_specs=[pl....  82.3 us

profile of v4, /device:TPU:1, one launch (start us, length us, event | category | flops | bytes accessed | tf_op | source)
XLA Modules:
  0.0 84.3 jit_solution(10260820659382856927)
XLA Ops:
  0.6 82.3 %shard_map.95 = (f32[16,16,128]{2,1,0:T(8,128)S(1)}, f32[16,16,128]{2,1,0:T(8,128)S(1)}) custom-call(f32[16,16,128]{2,1,0:T(8,128)} %refs_0_.1, f32[16,16,128]{2,1,0:T(8,128)} %refs_1_.1, f32[16,16,128]{2,1,0:T(8,128)} %refs_2_.1, f32[16,16,128]{2,1,0:T(8,128)} %refs_3_.1, f32[16,16,128]{2,1,0:T(8,128)} %refs_4_.1, f32[3,128,128]{2,1,0:T(8,128)} %constant.6.clone.refs_5_, ...), custom_call_target="tpu_custom_call" | custom-call | tf_op jit(solution)/shard_map/pallas_call | solution.py:542
  83.0 0.7 copy.12
  83.6 0.7 copy.13

commit v5 on v4

--- a/solution.py
+++ b/solution.py
@@ -113,7 +113,7 @@
 def kernel(
     dims, xwidth,
     src_hbm, mx_hbm, my_hbm, mz_hbm, mass_hbm, mats_hbm, facs_hbm, lanes_hbm,
-    sol_ref, res_ref,
+    out_ref,
     src_ref, mx_ref, my_ref, mz_ref, mass_ref, mats_ref, facs_ref, lanes_ref,
     jac, T, Y, L, V, Z, A, YS, PS, PR, FC, XF, YF, ZF, XZ, RB, acc, count, row_a, row_b, buf_a, buf_b,
     ssem, rsem, ssem_a, rsem_a, ssem_b, rsem_b, lsem,
@@ -155,6 +155,13 @@
     def far_first(n):
         return sorted(range(1, n), key=lambda k: abs(2 * k - n))
 
+    barrier = pltpu.get_barrier_semaphore()
+
+    def greet(group, n):
+        for k in far_first(n):
+            pl.semaphore_signal(barrier, inc=1, device_id=group(k), device_id_type=MESH)
+
+    greet(dev_b, ring)
     loads = [
         pltpu.make_async_copy(a, b, lsem.at[i])
         for i, (a, b) in enumerate(
@@ -170,22 +177,15 @@
             )
         )
     ]
-    for load in loads:
-        load.start()
     for ref in (XF, YF, ZF, XZ, RB):
         ref[0] = jnp.zeros(ref.shape[1:], jnp.float32)
-    barrier = pltpu.get_barrier_semaphore()
-
-    def greet(group, n):
-        for k in far_first(n):
-            pl.semaphore_signal(barrier, inc=1, device_id=group(k), device_id_type=MESH)
-
-    greet(dev_b, ring)
     for o in NEAR:
         @pl.when(exists(o))
         def _(o=o):
             pl.semaphore_signal(barrier, inc=1, device_id=dev(o), device_id_type=MESH)
     greet(dev_a, plane)
+    for load in loads:
+        load.start()
     sides = [1 + (at > 0).astype(jnp.int32) + (at < n - 1).astype(jnp.int32) for at, n in here.values()]
     n_near = sides[0] * sides[1] * sides[2] - 1
 
@@ -455,8 +455,7 @@
         add_rows(Z.at[j + 2], d_base)
         add_rows(V.at[j + 1], d_smooth)
 
-    sums = jnp.sum(acc[...], axis=1)
-    sums = jnp.sum(sums, axis=1, keepdims=True)
+    sums = jnp.sum(jnp.sum(acc[...], axis=1), axis=1, keepdims=True)
     pick = lax.broadcasted_iota(jnp.int32, (24, 128), 0) == lax.broadcasted_iota(jnp.int32, (24, 128), 1)
 
     def share(row, buf, me, group, n, ss, rs, values):
@@ -498,8 +497,10 @@
 
     H = [[value(4 * max(i, j) + min(i, j)) for j in range(ITERS)] for i in range(ITERS)]
     g = [value(16 + i) for i in range(ITERS)]
+    inverse = []
     for k in range(ITERS):
         inv = 1.0 / H[k][k]
+        inverse.append(inv)
         for i in range(k + 1, ITERS):
             f = H[i][k] * inv
             for j in range(k + 1, ITERS):
@@ -510,7 +511,7 @@
         s = g[k]
         for j in range(k + 1, ITERS):
             s = s - H[k][j] * y[j]
-        y[k] = s / H[k][k]
+        y[k] = s * inverse[k]
 
     wide = [jnp.broadcast_to(c, (8, 128))[None] for c in y]
     total = wide[0] * V[0].reshape(32, 8, 128)
@@ -518,8 +519,8 @@
     for j in range(1, ITERS):
         total = total + wide[j] * V[j].reshape(32, 8, 128)
         rest = rest - wide[j] * A[j].reshape(32, 8, 128)
-    sol_ref[...] = total.reshape(16, 16, 128)
-    res_ref[...] = rest.reshape(16, 16, 128)
+    out_ref[0] = total.reshape(16, 16, 128)
+    out_ref[1] = rest.reshape(16, 16, 128)
 
     left_b()
 
@@ -539,11 +540,11 @@
             kernel(dims, xwidth, *refs)
 
         mats, facs, lanes = constants()
-        return pl.pallas_call(
+        both = pl.pallas_call(
             run,
-            out_shape=[pltpu.VMEM(block, f32)] * 2,
+            out_shape=pltpu.VMEM((2,) + block, f32),
             in_specs=[pl.BlockSpec(memory_space=pltpu.HBM)] * 8,
-            out_specs=[vmem] * 2,
+            out_specs=vmem,
             scratch_shapes=[
                 *[pltpu.VMEM(block, f32)] * 5,
                 pltpu.VMEM(mats.shape, f32),
@@ -583,6 +584,7 @@
                 collective_id=0, has_side_effects=True, vmem_limit_bytes=32 * 1024 * 1024
             ),
         )(*(pltpu.with_memory_space_constraint(a, pltpu.HBM) for a in (*args, jnp.asarray(mats), jnp.asarray(facs), jnp.asarray(lanes))))
+        return both[0], both[1]
 
     spec = P(*AXES)
     return jax.shard_map(

time: 84.4 us -> 83.9 us (level)
    unnamed x2 -> x0, local copies, waits for them, and re-layouts: 1.31 us -> none
where the time goes in v5:
time: 83.9 us; the launch traced here: 83.7 us
  Pallas kernels  82.3 us (98%)
    pallas_call x1, Pallas kernels, body(): pl.pallas_call(run, out_shape=pltpu.VMEM((2,) + block, f32), in_specs=[pl...  82.3 us

profile of v5, /device:TPU:1, one launch (start us, length us, event | category | flops | bytes accessed | tf_op | source)
XLA Modules:
  0.0 83.7 jit_solution(1202033357747903205)
XLA Ops:
  0.6 82.3 %shard_map.95 = f32[2,16,16,128]{3,2,1,0:T(8,128)S(1)} custom-call(f32[16,16,128]{2,1,0:T(8,128)} %refs_0_.1, f32[16,16,128]{2,1,0:T(8,128)} %refs_1_.1, f32[16,16,128]{2,1,0:T(8,128)} %refs_2_.1, f32[16,16,128]{2,1,0:T(8,128)} %refs_3_.1, f32[16,16,128]{2,1,0:T(8,128)} %refs_4_.1, f32[3,128,128]{2,1,0:T(8,128)} %constant.6.clone.refs_5_, ...), custom_call_target="tpu_custom_call" | custom-call | tf_op jit(solution)/shard_map/pallas_call | solution.py:543
  83.0 0.7 slice_bitcast_fusion
